TPU v7x, 256 devices: a whole 4x4x8 slice. The times are simulated.
256 devices in a mesh: facet: 16 (over z, x_hi), strip: 16 (over x_lo, y, core).
Axes of the slice: x: 4 (x_hi: 2, x_lo: 2; x = x_hi * 2 + x_lo), y: 4, z: 8, core: 2. Of those that a mesh axis runs over, the one named last changes fastest.
Arguments:
- facets: bfloat16 [16, 2, 512, 8192], P('facet', None, None, 'strip'), may hold values from -6 to 6
- offsets: int32 [4], replicated, may hold values from 0 to 32767
- visibilities: float32 [2, 512, 2048], P(None, 'strip', 'facet'), may hold values from -24 to 24
- weights: float32 [512, 2048], P('strip', 'facet'), may hold values from 0.1 to 1
- mask: int32 [512, 2048], P('strip', 'facet'), may hold values 0 or 1
Outputs:
- facet_update: bfloat16 [16, 2, 512, 8192], P('facet', None, None, 'strip')
Inputs may be any that keep to these rules, and one draw needn't show every extreme that they name: `mask`: 1 where the cell holds a sampled visibility.
All inputs are finite; a program needn't handle non-finite values. No bound on the sum of `mask` on one device may be relied on, other than what follows from the above.
Results may differ from a plain program's by a relative error of at most 0.0058.
Values may be sent and summed in bfloat16 or wider, within the bound.
A program may use at most 128 MiB of HBM per device.

v0:
```python
import math

import jax
import jax.numpy as jnp
from jax import lax
from jax.sharding import PartitionSpec as P

NG = 32768
XM = 8192
SG = 512
NSUB = 4
FROWS = 4


def residue_angle(count):
    return count.astype(jnp.float32) * (2.0 * math.pi / NG)


def dft_kernel(start, rows):
    positions = start + jnp.arange(rows, dtype=jnp.int32)
    cells = jnp.arange(SG, dtype=jnp.int32)
    angle = residue_angle(positions[:, None] * cells[None, :] % NG)
    return jnp.concatenate([jnp.cos(angle), jnp.sin(angle)], axis=1).astype(jnp.bfloat16)


def row_angles(start, rows, offsets):
    positions = start + jnp.arange(rows, dtype=jnp.int32)
    return residue_angle(offsets[:, None] * positions[None, :] % NG)


def column_angles(facet_index, offsets):
    centre = (facet_index % FROWS * XM + NG // 2) % NG
    cells = jnp.arange(SG, dtype=jnp.int32)
    return residue_angle((cells[None, :] * centre % NG + offsets[:, None] * centre % NG) % NG)


def forward(data, start, facet_index, offsets, kernel_table):
    columns = data.shape[1]
    rows = data.shape[2]
    phi = row_angles(start, rows, offsets)[:, None, :]
    cos_phi = jnp.cos(phi)
    sin_phi = jnp.sin(phi)
    real_part = data[0].astype(jnp.float32)[None]
    imag_part = data[1].astype(jnp.float32)[None]
    twisted = jnp.stack(
        [real_part * cos_phi + imag_part * sin_phi, imag_part * cos_phi - real_part * sin_phi],
        axis=1,
    ).astype(jnp.bfloat16)
    spectra = jnp.dot(twisted.reshape(-1, rows), kernel_table, preferred_element_type=jnp.float32)
    spectra = spectra.reshape(NSUB, 2, columns, 2, SG)
    spectrum_real = spectra[:, 0, :, 0] + spectra[:, 1, :, 1]
    spectrum_imag = spectra[:, 1, :, 0] - spectra[:, 0, :, 1]
    psi = column_angles(facet_index, offsets)[:, None, :]
    cos_psi = jnp.cos(psi)
    sin_psi = jnp.sin(psi)
    scale = 1.0 / math.sqrt(XM)
    result_real = (spectrum_real * cos_psi + spectrum_imag * sin_psi) * scale
    result_imag = (spectrum_imag * cos_psi - spectrum_real * sin_psi) * scale
    stacked = jnp.stack([result_real, result_imag])
    return stacked.transpose(0, 2, 1, 3).reshape(2, columns, NSUB * SG)


def adjoint(residual, start, facet_index, offsets, kernel_table):
    columns = residual.shape[1]
    rows = kernel_table.shape[0]
    values = residual.astype(jnp.float32).reshape(2, columns, NSUB, SG).transpose(0, 2, 1, 3)
    psi = column_angles(facet_index, offsets)[:, None, :]
    cos_psi = jnp.cos(psi)
    sin_psi = jnp.sin(psi)
    first = values[0] * cos_psi - values[1] * sin_psi
    second = values[1] * cos_psi + values[0] * sin_psi
    untwisted = jnp.stack([first, second], axis=1).astype(jnp.bfloat16)
    images = jnp.einsum(
        "mj,xpj->pmx",
        untwisted.reshape(-1, SG),
        kernel_table.reshape(rows, 2, SG),
        preferred_element_type=jnp.float32,
    )
    images = images.reshape(2, NSUB, 2, columns, rows)
    image_real = images[0, :, 0] - images[1, :, 1]
    image_imag = images[0, :, 1] + images[1, :, 0]
    phi = row_angles(start, rows, offsets)[:, None, :]
    cos_phi = jnp.cos(phi)
    sin_phi = jnp.sin(phi)
    scale = 1.0 / math.sqrt(XM)
    total_real = jnp.sum(image_real * cos_phi - image_imag * sin_phi, axis=0) * scale
    total_imag = jnp.sum(image_imag * cos_phi + image_real * sin_phi, axis=0) * scale
    return jnp.stack([total_real, total_imag])


def weigh(model, visibilities, weights, mask):
    factor = weights * mask.astype(jnp.float32)
    return (factor[None] * (visibilities - model)).astype(jnp.bfloat16)


def on_device(facets, offsets, visibilities, weights, mask):
    facet_index = lax.axis_index("facet")
    strip_count = lax.axis_size("strip")
    facet_count = lax.axis_size("facet")
    rows_local = facets.shape[3]
    start = lax.axis_index("strip") * rows_local
    kernel_table = dft_kernel(start, rows_local)
    contribution = forward(facets[0], start, facet_index, offsets, kernel_table)
    slice_cols = contribution.shape[1] // strip_count
    slice_freq = contribution.shape[2] // facet_count
    arranged = contribution.reshape(2, strip_count, slice_cols, facet_count, slice_freq)
    arranged = arranged.transpose(0, 3, 1, 2, 4).reshape(
        2, facet_count * strip_count * slice_cols, slice_freq
    )
    model = lax.psum_scatter(arranged, ("facet", "strip"), scatter_dimension=1, tiled=True)
    residual = weigh(model, visibilities, weights, mask)
    gathered = lax.all_gather(residual, ("facet", "strip"), axis=1, tiled=True)
    gathered = gathered.reshape(2, facet_count, strip_count, slice_cols, slice_freq)
    gathered = gathered.transpose(0, 2, 3, 1, 4).reshape(
        2, strip_count * slice_cols, facet_count * slice_freq
    )
    update = adjoint(gathered, start, facet_index, offsets, kernel_table).astype(jnp.bfloat16)
    return update[None]


def solution(mesh):
    placed = (
        P("facet", None, None, "strip"),
        P(),
        P(None, "strip", "facet"),
        P("strip", "facet"),
        P("strip", "facet"),
    )
    return jax.shard_map(
        on_device,
        mesh=mesh,
        in_specs=placed,
        out_specs=P("facet", None, None, "strip"),
        check_vma=False,
    )
```

profile of v0, /device:TPU:1, one launch (start us, length us, event | category | flops | bytes accessed | tf_op | source)
XLA Modules:
  0.0 1553.1 jit_solution(6056781321906896631)
XLA Ops:
  6.5 0.0 reduce-scatter.2.cloned.1.call-start
  6.5 0.7 and_select_fusion
  7.2 0.8 fusion.34
  8.0 4.4 cosine_convert_fusion
  12.4 1.5 bitcast_convert_fusion.1
  13.9 0.2 fusion.32
  14.1 0.1 pad_maximum_fusion.1
  14.2 1.1 add_convert_fusion.1
  15.3 4.6 fusion.3
  19.9 3.0 add_multiply_fusion
  22.8 4.3 maximum_bitcast_fusion
  27.1 12.0 copy.35
  39.1 10.3 reshape_reshape.3
  49.4 9.1 copy.36
  58.4 0.0 copy-start.1
  58.5 0.0 copy-start.2
  58.5 0.0 copy-start
  58.5 0.0 reduce-scatter.2.cloned.1.call-update
  58.5 0.0 all-gather.2.cloned.1.call-start
  58.5 0.6 copy-done.1
  59.2 0.0 copy-done.2
  59.2 1276.8 %reduce-scatter.2.cloned.1.call-done = f32[2,32,128]{2,1,0:T(8,128)} async-done(((f32[2,8192,128]{2,1,0:T(8,128)}), f32[2,32,128]{2,1,0:T(8,128)}) %reduce-scatter.2.cloned.1.call-update) | async-done | bytes 32784 | tf_op jit(solution)/shard_map/reduce_scatter | solution.py:110
  1336.0 0.0 copy-done
  1336.0 1.4 multiply_convert_fusion.2
  1337.4 0.0 all-gather.2.cloned.1.call-update
  1337.4 0.1 copy.41
  1337.5 0.1 copy.44
  1337.7 5.1 cosine_convert_fusion.1
  1342.8 109.5 %all-gather.2.cloned.1.call-done = bf16[2,8192,128]{2,1,0:T(8,128)(2,1)} async-done(((bf16[2,32,128]{2,1,0:T(8,128)(2,1)}), bf16[2,8192,128]{2,1,0:T(8,128)(2,1)}) %all-gather.2.cloned.1.call-update) | async-done | bytes 4194320 | tf_op jit(solution)/shard_map/all_gather | solution.py:112
  1452.3 10.3 copy.79
  1462.6 9.9 reshape.458
  1472.5 4.6 subtract_convert_fusion
  1477.1 3.0 pad_maximum_fusion
  1480.0 0.8 copy.38
  1480.9 8.4 convolution_bitcast_fusion
  1489.3 22.0 %reshape.455 = f32[2,4,2,512,512]{3,2,1,4,0:T(2,128)} reshape(f32[2,4096,512]{1,2,0:T(8,128)} %convolution_bitcast_fusion) | data formatting | bytes 33554432 | tf_op jit(solution)/shard_map/reshape | solution.py:79
  1511.3 20.7 %fusion.39 = (f32[1,4,1,512,512]{3,2,1,4,0:T(1,128)S(1)}, f32[1,4,1,512,512]{3,2,1,4,0:T(1,128)S(1)}, f32[1,4,1,512,512]{3,2,1,4,0:T(1,128)S(1)}, f32[1,4,1,512,512]{3,2,1,4,0:T(1,128)S(1)}) fusion(f32[2,4,2,512,512]{3,2,1,4,0:T(2,128)} %reshape.455), kind=kLoop, calls=%fused_computation.94 | loop fusion | bytes 33554432 | tf_op jit(solution)/shard_map/slice | solution.py:81
  1532.0 12.1 subtract_reduce_fusion
  1544.1 0.3 fusion.23
  1544.4 0.1 pad_maximum_fusion.2
  1544.5 1.3 copy.45
  (3 shorter events, 0.0 us)
Async XLA Ops:
  6.5 1329.5 %reduce-scatter.2.cloned.1.call-start = ((), (), s32[]{:S(2)}) async-start(), calls=%async_computation.1 | async-start | bytes 8421376 | tf_op jit(solution)/shard_map/reduce_scatter | solution.py:110
  58.4 0.7 copy-start.1
  58.5 0.7 copy-start.2
  58.5 1277.5 %copy-start = (f32[2,32,128]{2,1,0:T(8,128)S(1)}, f32[2,32,128]{2,1,0:T(8,128)}, u32[]{:S(2)}) copy-start(f32[2,32,128]{2,1,0:T(8,128)} %param.7) | copy-start | bytes 98308
  58.5 1393.9 %all-gather.2.cloned.1.call-start = ((), (), s32[]{:S(2)}) async-start(), calls=%async_computation.2 | async-start | bytes 4210688 | tf_op jit(solution)/shard_map/all_gather | solution.py:112
Sparse Core Ops, SparseCore 0:
  58.6 1277.3 reduce-scatter.1
  1340.4 111.8 all-gather.1
where the time goes:
time: 1560 us; the launch traced here: 1550 us
  waiting for transfers between devices  1390 us (89%)
  local copies, waits for them, and re-layouts  97.3 us (6%)
  other arithmetic  42.5 us (3%)
    reduce_scatter x1, waiting for transfers between devices, on_device(): lax.psum_scatter(arranged, ('facet', 'strip'), scatter_dimension=1, tiled...  1280 us
    all_gather x1, waiting for transfers between devices, on_device(): gathered = lax.all_gather(residual, ('facet', 'strip'), axis=1, tiled=True)  110 us
  transfers between devices with their start and end apart: 2, of which 2 were waited for; matrix products, arithmetic and copies ran while one was open for 0% of the time, Pallas kernels for 0%

commit v1 on v0

v1 whole, which is shorter than its diff:
```python
import functools
import math

import jax
import jax.numpy as jnp
from jax import lax
from jax.experimental import pallas as pl
from jax.experimental.pallas import tpu as pltpu
from jax.sharding import PartitionSpec as P

NSUB = 4
FROWS = 4
MESH = pl.DeviceIdType.MESH


def turn(count, cells):
    quarter = cells // 4
    shift = quarter.bit_length() - 1
    quadrant = (count + quarter // 2) >> shift
    angle = (count - (quadrant << shift)).astype(jnp.float32) * (2.0 * math.pi / cells)
    square = angle * angle
    sine = angle * (1.0 + square * (-1.0 / 6 + square * (1.0 / 120 + square * (-1.0 / 5040 + square * (1.0 / 362880)))))
    cosine = 1.0 + square * (-0.5 + square * (1.0 / 24 + square * (-1.0 / 720 + square * (1.0 / 40320))))
    odd = (quadrant & 1) == 1
    first = jnp.where(odd, sine, cosine)
    second = jnp.where(odd, cosine, sine)
    cos_value = jnp.where(((quadrant + 1) & 2) == 2, -first, first)
    sin_value = jnp.where((quadrant & 2) == 2, -second, second)
    return cos_value, sin_value


def quarter_turn(count):
    part = count & 3
    sign = jnp.where(part >= 2, -1.0, 1.0)
    even = (part & 1) == 0
    return jnp.where(even, sign, 0.0), jnp.where(even, 0.0, sign)


def kernel(
    nf, ns,
    facets, offsets, vis, weights, mask, out,
    parts, table, phase, lhs, acc, factor, vis_here, factor_here, partial, partials, resid, result,
    a_send, a_recv, v_send, v_recv, c_send, c_recv, e_send, e_recv, g_send, g_recv, local_sem,
):
    f = lax.axis_index("facet")
    t = lax.axis_index("strip")
    cols, rows = parts.shape[2], parts.shape[3]
    cells = FROWS * rows * ns
    half = table.shape[1] // 2
    chunk = partial.shape[3]
    chunks = half // chunk
    scale = 1.0 / math.sqrt(rows * ns)
    start = t * rows
    apart = f != t

    def facet_peer(i):
        return lax.rem(f + i, nf)

    def strip_peer(i):
        return lax.rem(t + i, ns)

    barrier = pltpu.get_barrier_semaphore()

    def greet_facet(i, _):
        pl.semaphore_signal(barrier, inc=1, device_id=(facet_peer(i), t), device_id_type=MESH)
        return 0

    def greet_strip(i, _):
        pl.semaphore_signal(barrier, inc=1, device_id=(f, strip_peer(i)), device_id_type=MESH)
        return 0

    lax.fori_loop(1, nf, greet_facet, 0)
    lax.fori_loop(1, ns, greet_strip, 0)

    @pl.when(apart)
    def _():
        pl.semaphore_signal(barrier, inc=1, device_id=(t, f), device_id_type=MESH)

    pl.semaphore_wait(barrier, nf + ns - 2 + apart.astype(jnp.int32))

    def facet_columns(g):
        return pl.ds(pl.multiple_of(g * cols, cols), cols)

    def send_part(peer):
        return pltpu.make_async_remote_copy(
            src_ref=facets.at[0, :, facet_columns(peer), :], dst_ref=parts.at[f],
            send_sem=a_send.at[peer], recv_sem=a_recv.at[f], device_id=(peer, t), device_id_type=MESH)

    def arrive_part(peer):
        return pltpu.make_async_remote_copy(
            src_ref=parts.at[peer], dst_ref=parts.at[peer],
            send_sem=a_send.at[peer], recv_sem=a_recv.at[peer], device_id=(peer, t), device_id_type=MESH)

    def start_part(i, _):
        send_part(facet_peer(i)).start()
        return 0

    lax.fori_loop(1, nf, start_part, 0)
    own_part = pltpu.make_async_copy(facets.at[0, :, facet_columns(f), :], parts.at[f], local_sem.at[0])
    own_part.start()

    factor[...] = weights[...] * mask[...].astype(jnp.float32)
    send_vis = pltpu.make_async_remote_copy(
        src_ref=vis, dst_ref=vis_here, send_sem=v_send.at[0], recv_sem=v_recv.at[0], device_id=(t, f), device_id_type=MESH)
    send_factor = pltpu.make_async_remote_copy(
        src_ref=factor, dst_ref=factor_here, send_sem=v_send.at[1], recv_sem=v_recv.at[1], device_id=(t, f), device_id_type=MESH)

    @pl.when(apart)
    def _():
        send_vis.start()
        send_factor.start()

    @pl.when(jnp.logical_not(apart))
    def _():
        vis_here[...] = vis[...]
        factor_here[...] = factor[...]

    with jax.named_scope("tables"):
        block = min(32, rows)

        def fill(i, _):
            base = pl.multiple_of(i * block, block)
            x = start + base + lax.broadcasted_iota(jnp.int32, (block, half), 0)
            j = lax.broadcasted_iota(jnp.int32, (block, half), 1)
            cos_value, sin_value = turn((x * j) & (cells - 1), cells)
            low = pl.ds(base, block)
            high = pl.ds(pl.multiple_of(rows + base, block), block)
            cos_value = cos_value.astype(jnp.bfloat16)
            table[low, :half] = cos_value
            table[high, half:] = cos_value
            table[low, half:] = (-sin_value).astype(jnp.bfloat16)
            table[high, :half] = sin_value.astype(jnp.bfloat16)
            return 0

        lax.fori_loop(0, rows // block, fill, 0)
        for s in range(NSUB):
            x = start + lax.broadcasted_iota(jnp.int32, (1, rows), 1)
            cos_value, sin_value = turn((x * offsets[s]) & (cells - 1), cells)
            phase[0, s] = cos_value
            phase[1, s] = sin_value

    def psi(r, s):
        j = lax.broadcasted_iota(jnp.int32, (1, half), 1)
        return quarter_turn((offsets[s] + j) * (r + 2))

    own_part.wait()

    def wait_part(i, _):
        arrive_part(facet_peer(i)).wait_recv()
        return 0

    lax.fori_loop(1, nf, wait_part, 0)

    def send_partial(peer):
        return pltpu.make_async_remote_copy(
            src_ref=partial.at[peer], dst_ref=partials.at[t],
            send_sem=c_send.at[peer], recv_sem=c_recv.at[t], device_id=(f, peer), device_id_type=MESH)

    def arrive_partial(peer):
        return pltpu.make_async_remote_copy(
            src_ref=partial.at[peer], dst_ref=partials.at[peer],
            send_sem=c_send.at[peer], recv_sem=c_recv.at[peer], device_id=(f, peer), device_id_type=MESH)

    with jax.named_scope("forward"):
        for r in range(FROWS):
            for comp in range(2):
                total = parts[r, comp].astype(jnp.float32)
                for g in range(r + FROWS, nf, FROWS):
                    total = total + parts[g, comp].astype(jnp.float32)
                result[r, comp] = total

        def forward_step(s, _):
            cos_phi = phase[0, s]
            sin_phi = phase[1, s]
            for r in range(FROWS):
                a = result[r, 0]
                b = result[r, 1]
                lhs[r * cols:(r + 1) * cols, :rows] = (a * cos_phi + b * sin_phi).astype(jnp.bfloat16)
                lhs[r * cols:(r + 1) * cols, rows:] = (b * cos_phi - a * sin_phi).astype(jnp.bfloat16)
            acc[...] = jnp.dot(lhs[...], table[...], preferred_element_type=jnp.float32)
            total_re = jnp.zeros((cols, half), jnp.float32)
            total_im = jnp.zeros((cols, half), jnp.float32)
            for r in range(FROWS):
                cos_psi, sin_psi = psi(r, s)
                re = acc[r * cols:(r + 1) * cols, :half]
                im = acc[r * cols:(r + 1) * cols, half:]
                total_re = total_re + re * cos_psi + im * sin_psi
                total_im = total_im + im * cos_psi - re * sin_psi
            total_re = (total_re * scale).astype(jnp.bfloat16)
            total_im = (total_im * scale).astype(jnp.bfloat16)
            for q in range(chunks):
                peer = s * chunks + q
                partial[peer, 0] = total_re[:, q * chunk:(q + 1) * chunk]
                partial[peer, 1] = total_im[:, q * chunk:(q + 1) * chunk]

                @pl.when(peer != t)
                def _():
                    send_partial(peer).start()
            return 0

        lax.fori_loop(0, NSUB, forward_step, 0)

    with jax.named_scope("weigh"):
        @pl.when(apart)
        def _():
            send_vis.wait_recv()
            send_factor.wait_recv()

        def add_partial(i, total):
            peer = strip_peer(i)
            arrive_partial(peer).wait_recv()
            return total + partials[peer].astype(jnp.float32)

        model = lax.fori_loop(1, ns, add_partial, partial[t].astype(jnp.float32))
        resid[t] = (factor_here[...][None] * (vis_here[...] - model)).astype(jnp.bfloat16)

    def send_resid(peer):
        return pltpu.make_async_remote_copy(
            src_ref=resid.at[t], dst_ref=resid.at[t],
            send_sem=e_send.at[peer], recv_sem=e_recv.at[t], device_id=(f, peer), device_id_type=MESH)

    def arrive_resid(peer):
        return pltpu.make_async_remote_copy(
            src_ref=resid.at[peer], dst_ref=resid.at[peer],
            send_sem=e_send.at[peer], recv_sem=e_recv.at[peer], device_id=(f, peer), device_id_type=MESH)

    def start_resid(i, _):
        send_resid(strip_peer(i)).start()
        return 0

    def wait_resid(i, _):
        arrive_resid(strip_peer(i)).wait_recv()
        return 0

    lax.fori_loop(1, ns, start_resid, 0)
    lax.fori_loop(1, ns, wait_resid, 0)

    def send_update(r, peer):
        return pltpu.make_async_remote_copy(
            src_ref=lhs_out(r), dst_ref=out.at[0, :, facet_columns(f), :],
            send_sem=g_send.at[peer], recv_sem=g_recv.at[f], device_id=(peer, t), device_id_type=MESH)

    def lhs_out(r):
        return parts.at[r]

    def own_update(r):
        return pltpu.make_async_copy(lhs_out(r), out.at[0, :, facet_columns(f), :], local_sem.at[1])

    def arrive_update(peer):
        return pltpu.make_async_remote_copy(
            src_ref=parts.at[0], dst_ref=out.at[0, :, facet_columns(peer), :],
            send_sem=g_send.at[peer], recv_sem=g_recv.at[peer], device_id=(peer, t), device_id_type=MESH)

    with jax.named_scope("adjoint"):
        def adjoint_step(r, _):
            for s in range(NSUB):
                cos_psi, sin_psi = psi(r, s)
                for q in range(chunks):
                    g = resid[s * chunks + q, 0].astype(jnp.float32)
                    h = resid[s * chunks + q, 1].astype(jnp.float32)
                    c = cos_psi[:, q * chunk:(q + 1) * chunk]
                    d = sin_psi[:, q * chunk:(q + 1) * chunk]
                    lhs[s * cols:(s + 1) * cols, q * chunk:(q + 1) * chunk] = (g * c - h * d).astype(jnp.bfloat16)
                    lhs[s * cols:(s + 1) * cols, half + q * chunk:half + (q + 1) * chunk] = (h * c + g * d).astype(jnp.bfloat16)
            acc[...] = lax.dot_general(
                lhs[...], table[...], (((1,), (1,)), ((), ())), preferred_element_type=jnp.float32)
            total_re = jnp.zeros((cols, rows), jnp.float32)
            total_im = jnp.zeros((cols, rows), jnp.float32)
            for s in range(NSUB):
                cos_phi = phase[0, s]
                sin_phi = phase[1, s]
                p = acc[s * cols:(s + 1) * cols, :rows]
                q = acc[s * cols:(s + 1) * cols, rows:]
                total_re = total_re + p * cos_phi - q * sin_phi
                total_im = total_im + q * cos_phi + p * sin_phi
            parts[r, 0] = (total_re * scale).astype(jnp.bfloat16)
            parts[r, 1] = (total_im * scale).astype(jnp.bfloat16)

            def start_update(i, _):
                peer = i * FROWS + r

                @pl.when(peer != f)
                def _():
                    send_update(r, peer).start()

                @pl.when(peer == f)
                def _():
                    own_update(r).start()
                return 0

            lax.fori_loop(0, nf // FROWS, start_update, 0)
            return 0

        lax.fori_loop(0, FROWS, adjoint_step, 0)

    with jax.named_scope("drain"):
        def drain_strip(i, _):
            peer = strip_peer(i)
            send_partial(peer).wait_send()
            send_resid(peer).wait_send()
            return 0

        def drain_facet(i, _):
            peer = facet_peer(i)
            send_part(peer).wait_send()
            send_update(0, peer).wait_send()
            arrive_update(peer).wait_recv()
            return 0

        lax.fori_loop(1, ns, drain_strip, 0)
        lax.fori_loop(1, nf, drain_facet, 0)
        own_update(0).wait()

        @pl.when(apart)
        def _():
            send_vis.wait_send()
            send_factor.wait_send()


def on_device(nf, ns, facets, offsets, visibilities, weights, mask):
    _, _, columns, rows = facets.shape
    cols = columns // nf
    frequencies = visibilities.shape[2] * nf
    half = frequencies // NSUB
    chunk = frequencies // ns
    vmem = pl.BlockSpec(memory_space=pltpu.VMEM)
    anywhere = pl.BlockSpec(memory_space=pl.ANY)
    dma = pltpu.SemaphoreType.DMA
    flops = 2 * 2 * FROWS * NSUB * cols * (2 * rows) * (2 * half)
    return pl.pallas_call(
        functools.partial(kernel, nf, ns),
        out_shape=jax.ShapeDtypeStruct(facets.shape, jnp.bfloat16),
        in_specs=[anywhere, pl.BlockSpec(memory_space=pltpu.SMEM), vmem, vmem, vmem],
        out_specs=anywhere,
        scratch_shapes=[
            pltpu.VMEM((nf, 2, cols, rows), jnp.bfloat16),
            pltpu.VMEM((2 * rows, 2 * half), jnp.bfloat16),
            pltpu.VMEM((2, NSUB, 1, rows), jnp.float32),
            pltpu.VMEM((NSUB * cols, 2 * max(half, rows)), jnp.bfloat16),
            pltpu.VMEM((NSUB * cols, 2 * max(half, rows)), jnp.float32),
            pltpu.VMEM(weights.shape, jnp.float32),
            pltpu.VMEM(visibilities.shape, jnp.float32),
            pltpu.VMEM(weights.shape, jnp.float32),
            pltpu.VMEM((ns, 2, cols, chunk), jnp.bfloat16),
            pltpu.VMEM((ns, 2, cols, chunk), jnp.bfloat16),
            pltpu.VMEM((ns, 2, cols, chunk), jnp.bfloat16),
            pltpu.VMEM((FROWS, 2, cols, rows), jnp.float32),
            dma((nf,)), dma((nf,)), dma((2,)), dma((2,)), dma((ns,)), dma((ns,)), dma((ns,)), dma((ns,)),
            dma((nf,)), dma((nf,)), dma((2,)),
        ],
        cost_estimate=pl.CostEstimate(flops=flops, bytes_accessed=4 * facets.size, transcendentals=0),
        compiler_params=pltpu.CompilerParams(
            collective_id=0, has_side_effects=True, vmem_limit_bytes=48 * 1024 * 1024),
    )(facets, offsets, visibilities, weights, mask)


def solution(mesh):
    placed = (
        P("facet", None, None, "strip"),
        P(),
        P(None, "strip", "facet"),
        P("strip", "facet"),
        P("strip", "facet"),
    )
    return jax.shard_map(
        functools.partial(on_device, mesh.shape["facet"], mesh.shape["strip"]),
        mesh=mesh,
        in_specs=placed,
        out_specs=P("facet", None, None, "strip"),
        check_vma=False,
    )
```

time: 1560 us -> 86.5 us (0.06)
  the two profiles are of different devices: /device:TPU:1 before, /device:TPU:253 now
where the time goes in v1:
time: 86.5 us; the launch traced here: 86.2 us
  Pallas kernels  81.1 us (94%)
  local copies, waits for them, and re-layouts  5.04 us (6%)
    pallas_call x1, Pallas kernels, on_device(): pl.pallas_call(functools.partial(kernel, nf, ns), out_shape=jax.ShapeDtyp...  81.1 us
    unnamed x11, local copies, waits for them, and re-layouts  5.04 us

profile of v1, /device:TPU:253, one launch (start us, length us, event | category | flops | bytes accessed | tf_op | source)
XLA Modules:
  0.0 86.2 jit_solution(5721773595079000485)
XLA Ops:
  0.0 0.0 copy-start
  0.0 1.2 %copy-done = bf16[1,2,512,512]{3,2,1,0:T(8,128)(2,1)S(1)} copy-done((bf16[1,2,512,512]{3,2,1,0:T(8,128)(2,1)S(1)}, bf16[1,2,512,512]{3,2,1,0:T(8,128)(2,1)}, u32[]{:S(2)}) %copy-start) | copy-done | bytes 1048600
  1.2 0.0 copy-start.1
  1.2 0.8 copy-done.1
  2.0 0.0 copy-start.2
  2.0 0.7 copy-done.2
  2.7 0.0 copy-start.3
  2.7 0.7 copy-done.3
  3.4 0.0 copy-start.4
  3.4 0.7 copy-done.4
  4.1 81.1 %shard_map.55 = bf16[1,2,512,512]{3,2,1,0:T(8,128)(2,1)S(1)} custom-call(bf16[1,2,512,512]{3,2,1,0:T(8,128)(2,1)S(1)} %copy-done, s32[4]{0:T(128)S(1)} %copy-done.4, f32[2,32,128]{2,1,0:T(8,128)S(1)} %copy-done.1, f32[32,128]{1,0:T(8,128)S(1)} %copy-done.2, s32[32,128]{1,0:T(8,128)S(1)} %copy-done.3), custom_call_target="tpu_custom_call" | custom-call | flops 2147483648 | bytes 2097152 | tf_op jit(solution)/shard_map/pallas_call | solution.py:330
  85.2 1.0 %copy.7 = bf16[1,2,512,512]{3,2,1,0:T(8,128)(2,1)} copy(bf16[1,2,512,512]{3,2,1,0:T(8,128)(2,1)S(1)} %shard_map.55) | data formatting | bytes 2097152
Async XLA Ops:
  0.0 1.2 %copy-start = (bf16[1,2,512,512]{3,2,1,0:T(8,128)(2,1)S(1)}, bf16[1,2,512,512]{3,2,1,0:T(8,128)(2,1)}, u32[]{:S(2)}) copy-start(bf16[1,2,512,512]{3,2,1,0:T(8,128)(2,1)} %facets.1) | copy-start | bytes 3145732
  1.2 0.8 copy-start.1
  2.0 0.7 copy-start.2
  2.7 0.7 copy-start.3
  3.4 0.7 copy-start.4

commit v2 on v1

v2 whole, which is shorter than its diff:
```python
import functools
import math

import jax
import jax.numpy as jnp
from jax import lax
from jax.experimental import pallas as pl
from jax.experimental.pallas import tpu as pltpu
from jax.sharding import PartitionSpec as P

NSUB = 4
FROWS = 4
MESH = pl.DeviceIdType.MESH


def turn(count, cells):
    quarter = cells // 4
    shift = quarter.bit_length() - 1
    quadrant = (count + quarter // 2) >> shift
    angle = (count - (quadrant << shift)).astype(jnp.float32) * (2.0 * math.pi / cells)
    square = angle * angle
    sine = angle * (1.0 + square * (-1.0 / 6 + square * (1.0 / 120 + square * (-1.0 / 5040 + square * (1.0 / 362880)))))
    cosine = 1.0 + square * (-0.5 + square * (1.0 / 24 + square * (-1.0 / 720 + square * (1.0 / 40320))))
    odd = (quadrant & 1) == 1
    first = jnp.where(odd, sine, cosine)
    second = jnp.where(odd, cosine, sine)
    cos_value = jnp.where(((quadrant + 1) & 2) == 2, -first, first)
    sin_value = jnp.where((quadrant & 2) == 2, -second, second)
    return cos_value, sin_value


def quarter_turn(count):
    part = count & 3
    sign = jnp.where(part >= 2, -1.0, 1.0)
    even = (part & 1) == 0
    return jnp.where(even, sign, 0.0), jnp.where(even, 0.0, sign)


PASSES = 2


def kernel(
    nf, ns,
    facets, offsets_in, vis, weights_in, mask_in, out,
    offsets, weights, mask, mine, relayed, joint, parts, table, phase, lhs, acc, factor, vis_here, factor_here, partial, partials, resid, sums, update,
    r_send, r_recv, a_send, a_recv, v_send, v_recv, c_send, c_recv, e_send, e_recv, g_send, f_send, g_recv, g_local, local_sem,
):
    f = lax.axis_index("facet")
    t = lax.axis_index("strip")
    cols, rows = parts.shape[4], parts.shape[5]
    cells = FROWS * rows * ns
    half = table.shape[1] // 2
    chunk = partial.shape[4]
    chunks = half // chunk
    scale = 1.0 / math.sqrt(rows * ns)
    start = t * rows
    apart = f != t

    depth = nf // 2
    z = lax.div(f, 2)
    x = lax.rem(f, 2)
    odd = lax.rem(z, 2)

    def facet_at(dz, side):
        return lax.rem(z + dz + depth, depth) * 2 + side

    def strip_peer(i):
        return lax.rem(t + i, ns)

    def columns_of(g, p):
        return pl.ds(pl.multiple_of((g * PASSES + p) * cols, cols), cols)

    barrier = pltpu.get_barrier_semaphore()

    def greet_strip(i, _):
        pl.semaphore_signal(barrier, inc=1, device_id=(f, strip_peer(i)), device_id_type=MESH)
        return 0

    for dz in (1, -1, 2, -2):
        for side in range(2):
            pl.semaphore_signal(barrier, inc=1, device_id=(facet_at(dz, side), t), device_id_type=MESH)
    pl.semaphore_signal(barrier, inc=1, device_id=(facet_at(0, 1 - x), t), device_id_type=MESH)
    lax.fori_loop(1, ns, greet_strip, 0)

    @pl.when(apart)
    def _():
        pl.semaphore_signal(barrier, inc=1, device_id=(t, f), device_id_type=MESH)

    get_offsets = pltpu.make_async_copy(offsets_in, offsets, local_sem.at[0])
    get_weights = pltpu.make_async_copy(weights_in, weights, local_sem.at[1])
    get_mask = pltpu.make_async_copy(mask_in, mask, local_sem.at[2])
    get_vis = pltpu.make_async_copy(vis, vis_here, local_sem.at[3])
    get_offsets.start()
    get_weights.start()
    get_mask.start()
    get_mine = pltpu.make_async_copy(facets.at[0], mine, local_sem.at[4])
    get_mine.start()

    pl.semaphore_wait(barrier, 9 + ns - 1 + apart.astype(jnp.int32))

    routes = (((1, 0), (1, 1), (2, 0)), ((-1, 0), (-1, 1), (-2, 1)))
    place = {1: 0, -1: 1, 2: 2, -2: 3, 0: 4}

    def relay(p, way, u):
        step = 2 - 4 * way
        dz, side = routes[way][u]
        return pltpu.make_async_remote_copy(
            src_ref=facets.at[0, :, columns_of(facet_at(dz + step, side), p), :], dst_ref=relayed.at[p, way, u],
            send_sem=r_send.at[p, way, u], recv_sem=r_recv.at[p, way, u],
            device_id=(facet_at(step, x), t), device_id_type=MESH)

    def joined(p, way, u):
        dz, side = routes[way][u]
        return pltpu.make_async_remote_copy(
            src_ref=joint.at[p, way, u], dst_ref=parts.at[p, place[dz], x],
            send_sem=a_send.at[p, 3 * way + u], recv_sem=a_recv.at[p, place[dz], x],
            device_id=(facet_at(dz, side), t), device_id_type=MESH)

    def direct(p, n):
        dz, side = ((2, 1), (-2, 0), (0, 1 - x))[n]
        peer = facet_at(dz, side)
        return pltpu.make_async_remote_copy(
            src_ref=facets.at[0, :, columns_of(peer, p), :], dst_ref=parts.at[p, place[dz], x],
            send_sem=a_send.at[p, 6 + n], recv_sem=a_recv.at[p, place[dz], x],
            device_id=(peer, t), device_id_type=MESH)

    def arrive_part(p, k, side):
        return pltpu.make_async_remote_copy(
            src_ref=parts.at[p, k, side], dst_ref=parts.at[p, k, side],
            send_sem=a_send.at[p, 0], recv_sem=a_recv.at[p, k, side],
            device_id=(facet_at(0, 1 - x), t), device_id_type=MESH)

    def start_relays(p):
        for u in range(3):
            for way in range(2):
                relay(p, way, u).start()
        for n in range(3):
            direct(p, n).start()

    def join(p):
        for u in range(3):
            for way in range(2):
                relay(p, way, u).wait_recv()
                own = mine[:, columns_of(facet_at(*routes[way][u]), p), :]
                joint[p, way, u] = (relayed[p, way, u].astype(jnp.float32) + own.astype(jnp.float32)).astype(jnp.bfloat16)
                joined(p, way, u).start()

    start_relays(0)
    get_weights.wait()
    get_mask.wait()
    factor[...] = weights[...] * mask[...].astype(jnp.float32)
    send_vis = pltpu.make_async_remote_copy(
        src_ref=vis, dst_ref=vis_here, send_sem=v_send.at[0], recv_sem=v_recv.at[0], device_id=(t, f), device_id_type=MESH)
    send_factor = pltpu.make_async_remote_copy(
        src_ref=factor, dst_ref=factor_here, send_sem=v_send.at[1], recv_sem=v_recv.at[1], device_id=(t, f), device_id_type=MESH)

    @pl.when(apart)
    def _():
        send_vis.start()
        send_factor.start()

    @pl.when(jnp.logical_not(apart))
    def _():
        get_vis.start()
        factor_here[...] = factor[...]
        get_vis.wait()

    get_offsets.wait()

    with jax.named_scope("tables"):
        block = min(32, rows)

        def fill(i, _):
            base = pl.multiple_of(i * block, block)
            row = start + base + lax.broadcasted_iota(jnp.int32, (block, half), 0)
            j = lax.broadcasted_iota(jnp.int32, (block, half), 1)
            cos_value, sin_value = turn((row * j) & (cells - 1), cells)
            low = pl.ds(base, block)
            high = pl.ds(pl.multiple_of(rows + base, block), block)
            cos_value = cos_value.astype(jnp.bfloat16)
            table[low, :half] = cos_value
            table[high, half:] = cos_value
            table[low, half:] = (-sin_value).astype(jnp.bfloat16)
            table[high, :half] = sin_value.astype(jnp.bfloat16)
            return 0

        lax.fori_loop(0, rows // block, fill, 0)
        for s in range(NSUB):
            row = start + lax.broadcasted_iota(jnp.int32, (1, rows), 1)
            cos_value, sin_value = turn((row * offsets[s]) & (cells - 1), cells)
            phase[0, s] = cos_value
            phase[1, s] = sin_value

    get_mine.wait()
    for p in range(PASSES):
        join(p)
        if p + 1 < PASSES:
            start_relays(p + 1)

    def psi(r, s):
        j = lax.broadcasted_iota(jnp.int32, (1, half), 1)
        return quarter_turn((offsets[s] + j) * (r + 2))

    def send_partial(peer, p):
        return pltpu.make_async_remote_copy(
            src_ref=partial.at[p, peer], dst_ref=partials.at[p, t],
            send_sem=c_send.at[p, peer], recv_sem=c_recv.at[p, t], device_id=(f, peer), device_id_type=MESH)

    def arrive_partial(peer, p):
        return pltpu.make_async_remote_copy(
            src_ref=partial.at[p, peer], dst_ref=partials.at[p, peer],
            send_sem=c_send.at[p, peer], recv_sem=c_recv.at[p, peer], device_id=(f, peer), device_id_type=MESH)

    def send_resid(peer, p):
        return pltpu.make_async_remote_copy(
            src_ref=resid.at[p, t], dst_ref=resid.at[p, t],
            send_sem=e_send.at[p, peer], recv_sem=e_recv.at[p, t], device_id=(f, peer), device_id_type=MESH)

    def arrive_resid(peer, p):
        return pltpu.make_async_remote_copy(
            src_ref=resid.at[p, peer], dst_ref=resid.at[p, peer],
            send_sem=e_send.at[p, peer], recv_sem=e_recv.at[p, peer], device_id=(f, peer), device_id_type=MESH)

    spread = ((1, 0), (1, 1), (-1, 0), (-1, 1), (2, 0), (2, 1), (-2, 0), (-2, 1), (0, 1 - x))
    passed = ((-1, 0, 2), (1, 0, -2), (-1, 1, 2), (1, 1, -2), (-2, 0, 2), (2, 1, -2))

    def residue_at(dz, side):
        return lax.rem(odd + dz + 2, 2) * 2 + side

    def send_update(p, n):
        dz, side = spread[n]
        return pltpu.make_async_remote_copy(
            src_ref=update.at[p, residue_at(dz, side)], dst_ref=out.at[0, :, columns_of(f, p), :],
            send_sem=g_send.at[p, n], recv_sem=g_recv.at[p, f],
            device_id=(facet_at(dz, side), t), device_id_type=MESH)

    def pass_on(p, n):
        dz, side, step = passed[n]
        block = out.at[0, :, columns_of(facet_at(dz, side), p), :]
        return pltpu.make_async_remote_copy(
            src_ref=block, dst_ref=block,
            send_sem=f_send.at[p, n], recv_sem=g_recv.at[p, facet_at(dz, side)],
            device_id=(facet_at(step, x), t), device_id_type=MESH)

    def own_update(p):
        return pltpu.make_async_copy(update.at[p, residue_at(0, x)], out.at[0, :, columns_of(f, p), :], g_local.at[p])

    def arrive_update(p, peer):
        return pltpu.make_async_remote_copy(
            src_ref=update.at[p, 0], dst_ref=out.at[0, :, columns_of(peer, p), :],
            send_sem=g_send.at[p, 0], recv_sem=g_recv.at[p, peer],
            device_id=(facet_at(0, 1 - x), t), device_id_type=MESH)

    def relay_updates(p):
        for n in range(6):
            dz, side, _ = passed[n]
            arrive_update(p, facet_at(dz, side)).wait_recv()
            pass_on(p, n).start()

    def forward(p):
        for k in range(4):
            for side in range(2):
                arrive_part(p, k, side).wait_recv()
        arrive_part(p, 4, 1 - x).wait_recv()
        parts[p, 4, x] = mine[:, columns_of(f, p), :]
        for side in range(2):
            same = residue_at(0, side)
            other = residue_at(1, side)
            two = parts[p, 2, side].astype(jnp.float32) + parts[p, 3, side].astype(jnp.float32)
            sums[same] = two + parts[p, 4, side].astype(jnp.float32)
            sums[other] = parts[p, 0, side].astype(jnp.float32) + parts[p, 1, side].astype(jnp.float32)
        for s in range(NSUB):
            cos_phi = phase[0, s]
            sin_phi = phase[1, s]
            for r in range(FROWS):
                a = sums[r, 0]
                b = sums[r, 1]
                row = (s * FROWS + r) * cols
                lhs[row:row + cols, :rows] = (a * cos_phi + b * sin_phi).astype(jnp.bfloat16)
                lhs[row:row + cols, rows:] = (b * cos_phi - a * sin_phi).astype(jnp.bfloat16)
        acc[...] = jnp.dot(lhs[...], table[...], preferred_element_type=jnp.float32)
        for s in range(NSUB):
            total_re = jnp.zeros((cols, half), jnp.float32)
            total_im = jnp.zeros((cols, half), jnp.float32)
            for r in range(FROWS):
                cos_psi, sin_psi = psi(r, s)
                row = (s * FROWS + r) * cols
                re = acc[row:row + cols, :half]
                im = acc[row:row + cols, half:]
                total_re = total_re + re * cos_psi + im * sin_psi
                total_im = total_im + im * cos_psi - re * sin_psi
            total_re = (total_re * scale).astype(jnp.bfloat16)
            total_im = (total_im * scale).astype(jnp.bfloat16)
            for q in range(chunks):
                peer = s * chunks + q
                partial[p, peer, 0] = total_re[:, q * chunk:(q + 1) * chunk]
                partial[p, peer, 1] = total_im[:, q * chunk:(q + 1) * chunk]

        def start_partial(i, _):
            send_partial(strip_peer(i), p).start()
            return 0

        lax.fori_loop(1, ns, start_partial, 0)

    def weigh(p):
        if p == 0:
            @pl.when(apart)
            def _():
                send_vis.wait_recv()
                send_factor.wait_recv()

        def add_partial(i, total):
            peer = strip_peer(i)
            arrive_partial(peer, p).wait_recv()
            return total + partials[p, peer].astype(jnp.float32)

        model = lax.fori_loop(1, ns, add_partial, partial[p, t].astype(jnp.float32))
        mine = slice(p * cols, (p + 1) * cols)
        resid[p, t] = (factor_here[mine][None] * (vis_here[:, mine] - model)).astype(jnp.bfloat16)

        def start_resid(i, _):
            send_resid(strip_peer(i), p).start()
            return 0

        lax.fori_loop(1, ns, start_resid, 0)

    def adjoint(p):
        def wait_resid(i, _):
            arrive_resid(strip_peer(i), p).wait_recv()
            return 0

        lax.fori_loop(1, ns, wait_resid, 0)
        for r in range(FROWS):
            for s in range(NSUB):
                cos_psi, sin_psi = psi(r, s)
                row = (r * NSUB + s) * cols
                for q in range(chunks):
                    g = resid[p, s * chunks + q, 0].astype(jnp.float32)
                    h = resid[p, s * chunks + q, 1].astype(jnp.float32)
                    c = cos_psi[:, q * chunk:(q + 1) * chunk]
                    d = sin_psi[:, q * chunk:(q + 1) * chunk]
                    lhs[row:row + cols, q * chunk:(q + 1) * chunk] = (g * c - h * d).astype(jnp.bfloat16)
                    lhs[row:row + cols, half + q * chunk:half + (q + 1) * chunk] = (h * c + g * d).astype(jnp.bfloat16)
        acc[...] = lax.dot_general(
            lhs[...], table[...], (((1,), (1,)), ((), ())), preferred_element_type=jnp.float32)
        for r in range(FROWS):
            total_re = jnp.zeros((cols, rows), jnp.float32)
            total_im = jnp.zeros((cols, rows), jnp.float32)
            for s in range(NSUB):
                cos_phi = phase[0, s]
                sin_phi = phase[1, s]
                row = (r * NSUB + s) * cols
                a = acc[row:row + cols, :rows]
                b = acc[row:row + cols, rows:]
                total_re = total_re + a * cos_phi - b * sin_phi
                total_im = total_im + b * cos_phi + a * sin_phi
            update[p, r, 0] = (total_re * scale).astype(jnp.bfloat16)
            update[p, r, 1] = (total_im * scale).astype(jnp.bfloat16)

        own_update(p).start()
        for n in range(9):
            send_update(p, n).start()

    with jax.named_scope("transforms"):
        forward(0)
        weigh(0)
        forward(1)
        adjoint(0)
        weigh(1)
        relay_updates(0)
        adjoint(1)
        relay_updates(1)

    with jax.named_scope("drain"):
        for p in range(PASSES):
            def drain_strip(i, _):
                peer = strip_peer(i)
                send_partial(peer, p).wait_send()
                send_resid(peer, p).wait_send()
                return 0

            lax.fori_loop(1, ns, drain_strip, 0)
            for u in range(3):
                for way in range(2):
                    relay(p, way, u).wait_send()
                    joined(p, way, u).wait_send()
                direct(p, u).wait_send()
            for n in range(9):
                send_update(p, n).wait_send()
            for n in range(6):
                pass_on(p, n).wait_send()
            own_update(p).wait()
            arrive_update(p, facet_at(0, 1 - x)).wait_recv()
            for dz, side in ((-2, 1), (2, 0), (3, 0), (3, 1), (-3, 0), (-3, 1), (4, 0), (4, 1)):
                arrive_update(p, facet_at(dz, side)).wait_recv()

        @pl.when(apart)
        def _():
            send_vis.wait_send()
            send_factor.wait_send()


def on_device(nf, ns, facets, offsets, visibilities, weights, mask):
    _, _, columns, rows = facets.shape
    cols = columns // nf // PASSES
    frequencies = visibilities.shape[2] * nf
    half = frequencies // NSUB
    chunk = frequencies // ns
    hbm = pl.BlockSpec(memory_space=pltpu.HBM)
    dma = pltpu.SemaphoreType.DMA
    flops = 2 * 2 * FROWS * NSUB * cols * PASSES * (2 * rows) * (2 * half)
    exchanged = (PASSES, ns, 2, cols, chunk)
    return pl.pallas_call(
        functools.partial(kernel, nf, ns),
        out_shape=jax.ShapeDtypeStruct(facets.shape, jnp.bfloat16),
        in_specs=[hbm] * 5,
        out_specs=hbm,
        scratch_shapes=[
            pltpu.SMEM(offsets.shape, jnp.int32),
            pltpu.VMEM(weights.shape, jnp.float32),
            pltpu.VMEM(mask.shape, jnp.int32),
            pltpu.VMEM((2, columns, rows), jnp.bfloat16),
            pltpu.VMEM((PASSES, 2, 3, 2, cols, rows), jnp.bfloat16),
            pltpu.VMEM((PASSES, 2, 3, 2, cols, rows), jnp.bfloat16),
            pltpu.VMEM((PASSES, 5, 2, 2, cols, rows), jnp.bfloat16),
            pltpu.VMEM((2 * rows, 2 * half), jnp.bfloat16),
            pltpu.VMEM((2, NSUB, 1, rows), jnp.float32),
            pltpu.VMEM((FROWS * NSUB * cols, 2 * max(half, rows)), jnp.bfloat16),
            pltpu.VMEM((FROWS * NSUB * cols, 2 * max(half, rows)), jnp.float32),
            pltpu.VMEM(weights.shape, jnp.float32),
            pltpu.VMEM(visibilities.shape, jnp.float32),
            pltpu.VMEM(weights.shape, jnp.float32),
            pltpu.VMEM(exchanged, jnp.bfloat16),
            pltpu.VMEM(exchanged, jnp.bfloat16),
            pltpu.VMEM(exchanged, jnp.bfloat16),
            pltpu.VMEM((FROWS, 2, cols, rows), jnp.float32),
            pltpu.VMEM((PASSES, FROWS, 2, cols, rows), jnp.bfloat16),
            dma((PASSES, 2, 3)), dma((PASSES, 2, 3)), dma((PASSES, 9)), dma((PASSES, 5, 2)), dma((2,)), dma((2,)),
            dma((PASSES, ns)), dma((PASSES, ns)), dma((PASSES, ns)), dma((PASSES, ns)),
            dma((PASSES, 9)), dma((PASSES, 6)), dma((PASSES, nf)), dma((PASSES,)), dma((5,)),
        ],
        cost_estimate=pl.CostEstimate(flops=flops, bytes_accessed=4 * facets.size, transcendentals=0),
        compiler_params=pltpu.CompilerParams(
            collective_id=0, has_side_effects=True, vmem_limit_bytes=62 * 1024 * 1024),
    )(facets, offsets, visibilities, weights, mask)


def solution(mesh):
    placed = (
        P("facet", None, None, "strip"),
        P(),
        P(None, "strip", "facet"),
        P("strip", "facet"),
        P("strip", "facet"),
    )
    return jax.shard_map(
        functools.partial(on_device, mesh.shape["facet"], mesh.shape["strip"]),
        mesh=mesh,
        in_specs=placed,
        out_specs=P("facet", None, None, "strip"),
        check_vma=False,
    )
```

time: 86.5 us -> 67 us (0.77)
  the two profiles are of different devices: /device:TPU:253 before, /device:TPU:24 now
where the time goes in v2:
time: 67 us; the launch traced here: 66.8 us
  Pallas kernels  64.5 us (96%)
  local copies, waits for them, and re-layouts  2.26 us (3%)
    pallas_call x1, Pallas kernels, on_device(): pl.pallas_call(functools.partial(kernel, nf, ns), out_shape=jax.ShapeDtyp...  64.5 us
    unnamed x1, local copies, waits for them, and re-layouts  2.26 us

profile of v2, /device:TPU:24, one launch (start us, length us, event | category | flops | bytes accessed | tf_op | source)
XLA Modules:
  0.0 66.8 jit_solution(11946850098807259463)
XLA Ops:
  0.0 64.5 %shard_map.55 = bf16[1,2,512,512]{3,2,1,0:T(8,128)(2,1)} custom-call(bf16[1,2,512,512]{3,2,1,0:T(8,128)(2,1)} %facets.1, s32[4]{0:T(128)} %offsets_in.1, f32[2,32,128]{2,1,0:T(8,128)} %vis.1, f32[32,128]{1,0:T(8,128)} %weights_in.1, s32[32,128]{1,0:T(8,128)} %mask_in.1), custom_call_target="tpu_custom_call" | custom-call | flops 2147483648 | bytes 2097152 | tf_op jit(solution)/shard_map/pallas_call | solution.py:413
  64.5 2.3 %copy.7 = bf16[1,2,512,512]{3,2,1,0:T(8,128)(2,1)} copy(bf16[1,2,512,512]{3,2,1,0:T(8,128)(2,1)} %shard_map.55) | data formatting | bytes 2097152

commit v3 on v2

--- a/solution.py
+++ b/solution.py
@@ -144,6 +144,11 @@
                 own = mine[:, columns_of(facet_at(*routes[way][u]), p), :]
                 joint[p, way, u] = (relayed[p, way, u].astype(jnp.float32) + own.astype(jnp.float32)).astype(jnp.bfloat16)
                 joined(p, way, u).start()
+                if p + 1 < PASSES:
+                    relay(p + 1, way, u).start()
+        if p + 1 < PASSES:
+            for n in range(3):
+                direct(p + 1, n).start()
 
     start_relays(0)
     get_weights.wait()
@@ -194,8 +199,6 @@
     get_mine.wait()
     for p in range(PASSES):
         join(p)
-        if p + 1 < PASSES:
-            start_relays(p + 1)
 
     def psi(r, s):
         j = lax.broadcasted_iota(jnp.int32, (1, half), 1)
@@ -441,8 +444,8 @@
         ],
         cost_estimate=pl.CostEstimate(flops=flops, bytes_accessed=4 * facets.size, transcendentals=0),
         compiler_params=pltpu.CompilerParams(
-            collective_id=0, has_side_effects=True, vmem_limit_bytes=62 * 1024 * 1024),
-    )(facets, offsets, visibilities, weights, mask)
+            collective_id=0, has_side_effects=True, vmem_limit_bytes=50 * 1024 * 1024),
+    )(*(pltpu.with_memory_space_constraint(value, pltpu.HBM) for value in (facets, offsets, visibilities, weights, mask)))
 
 
 def solution(mesh):

time: 67 us -> 65.4 us (0.976)
  the two profiles are of different devices: /device:TPU:24 before, /device:TPU:1 now
where the time goes in v3:
time: 65.4 us; the launch traced here: 65.2 us
  Pallas kernels  64.3 us (98%)
  local copies, waits for them, and re-layouts  0.97 us (1%)
    pallas_call x1, Pallas kernels, on_device(): pl.pallas_call(functools.partial(kernel, nf, ns), out_shape=jax.ShapeDtyp...  64.3 us

profile of v3, /device:TPU:1, one launch (start us, length us, event | category | flops | bytes accessed | tf_op | source)
XLA Modules:
  0.0 65.2 jit_solution(10582912507846473395)
XLA Ops:
  0.0 64.3 %shard_map.55 = bf16[1,2,512,512]{3,2,1,0:T(8,128)(2,1)S(1)} custom-call(bf16[1,2,512,512]{3,2,1,0:T(8,128)(2,1)} %facets.1, s32[4]{0:T(128)} %offsets_in.1, f32[2,32,128]{2,1,0:T(8,128)} %vis.1, f32[32,128]{1,0:T(8,128)} %weights_in.1, s32[32,128]{1,0:T(8,128)} %mask_in.1), custom_call_target="tpu_custom_call" | custom-call | flops 2147483648 | bytes 2097152 | tf_op jit(solution)/shard_map/pallas_call | solution.py:416
  64.3 1.0 %copy.7 = bf16[1,2,512,512]{3,2,1,0:T(8,128)(2,1)} copy(bf16[1,2,512,512]{3,2,1,0:T(8,128)(2,1)S(1)} %shard_map.55) | data formatting | bytes 2097152

commit v4 on v3

--- a/solution.py
+++ b/solution.py
@@ -105,7 +105,7 @@
         step = 2 - 4 * way
         dz, side = routes[way][u]
         return pltpu.make_async_remote_copy(
-            src_ref=facets.at[0, :, columns_of(facet_at(dz + step, side), p), :], dst_ref=relayed.at[p, way, u],
+            src_ref=mine.at[:, columns_of(facet_at(dz + step, side), p), :], dst_ref=relayed.at[p, way, u],
             send_sem=r_send.at[p, way, u], recv_sem=r_recv.at[p, way, u],
             device_id=(facet_at(step, x), t), device_id_type=MESH)
 
@@ -120,7 +120,7 @@
         dz, side = ((2, 1), (-2, 0), (0, 1 - x))[n]
         peer = facet_at(dz, side)
         return pltpu.make_async_remote_copy(
-            src_ref=facets.at[0, :, columns_of(peer, p), :], dst_ref=parts.at[p, place[dz], x],
+            src_ref=mine.at[:, columns_of(peer, p), :], dst_ref=parts.at[p, place[dz], x],
             send_sem=a_send.at[p, 6 + n], recv_sem=a_recv.at[p, place[dz], x],
             device_id=(peer, t), device_id_type=MESH)
 
@@ -150,6 +150,7 @@
             for n in range(3):
                 direct(p + 1, n).start()
 
+    get_mine.wait()
     start_relays(0)
     get_weights.wait()
     get_mask.wait()
@@ -196,7 +197,6 @@
             phase[0, s] = cos_value
             phase[1, s] = sin_value
 
-    get_mine.wait()
     for p in range(PASSES):
         join(p)
 
@@ -230,10 +230,13 @@
     def residue_at(dz, side):
         return lax.rem(odd + dz + 2, 2) * 2 + side
 
+    def slot_of(dz, side):
+        return (0 if dz in (1, -1) else 2) + side
+
     def send_update(p, n):
         dz, side = spread[n]
         return pltpu.make_async_remote_copy(
-            src_ref=update.at[p, residue_at(dz, side)], dst_ref=out.at[0, :, columns_of(f, p), :],
+            src_ref=update.at[p, slot_of(dz, side)], dst_ref=out.at[0, :, columns_of(f, p), :],
             send_sem=g_send.at[p, n], recv_sem=g_recv.at[p, f],
             device_id=(facet_at(dz, side), t), device_id_type=MESH)
 
@@ -246,7 +249,7 @@
             device_id=(facet_at(step, x), t), device_id_type=MESH)
 
     def own_update(p):
-        return pltpu.make_async_copy(update.at[p, residue_at(0, x)], out.at[0, :, columns_of(f, p), :], g_local.at[p])
+        return pltpu.make_async_copy(update.at[p, slot_of(0, x)], out.at[0, :, columns_of(f, p), :], g_local.at[p])
 
     def arrive_update(p, peer):
         return pltpu.make_async_remote_copy(
@@ -299,11 +302,9 @@
                 partial[p, peer, 0] = total_re[:, q * chunk:(q + 1) * chunk]
                 partial[p, peer, 1] = total_im[:, q * chunk:(q + 1) * chunk]
 
-        def start_partial(i, _):
-            send_partial(strip_peer(i), p).start()
-            return 0
-
-        lax.fori_loop(1, ns, start_partial, 0)
+                @pl.when(peer != t)
+                def _():
+                    send_partial(peer, p).start()
 
     def weigh(p):
         if p == 0:
@@ -335,7 +336,7 @@
         lax.fori_loop(1, ns, wait_resid, 0)
         for r in range(FROWS):
             for s in range(NSUB):
-                cos_psi, sin_psi = psi(r, s)
+                cos_psi, sin_psi = psi(residue_at(1 - r // 2, r % 2), s)
                 row = (r * NSUB + s) * cols
                 for q in range(chunks):
                     g = resid[p, s * chunks + q, 0].astype(jnp.float32)
@@ -359,10 +360,11 @@
                 total_im = total_im + b * cos_phi + a * sin_phi
             update[p, r, 0] = (total_re * scale).astype(jnp.bfloat16)
             update[p, r, 1] = (total_im * scale).astype(jnp.bfloat16)
-
+            for n in ((0, 2), (1, 3), (4, 6), (5, 7))[r]:
+                send_update(p, n).start()
+
+        send_update(p, 8).start()
         own_update(p).start()
-        for n in range(9):
-            send_update(p, n).start()
 
     with jax.named_scope("transforms"):
         forward(0)

time: 65.4 us -> 64.6 us (0.988); the launches traced: 65.2 us -> 63.5 us
  Pallas kernels: 64.3 us -> 62.6 us
    pallas_call x1, Pallas kernels: 64.3 us -> 62.6 us  [on_device(): pl.pallas_call(functools.partial(kernel, nf, ns), out_shape=jax.ShapeDtyp...]
where the time goes in v4:
time: 64.6 us; the launch traced here: 63.5 us
  Pallas kernels  62.6 us (97%)
  local copies, waits for them, and re-layouts  0.97 us (2%)
    pallas_call x1, Pallas kernels, on_device(): pl.pallas_call(functools.partial(kernel, nf, ns), out_shape=jax.ShapeDtyp...  62.6 us

profile of v4, /device:TPU:1, one launch (start us, length us, event | category | flops | bytes accessed | tf_op | source)
XLA Modules:
  0.0 63.5 jit_solution(14609603130917714749)
XLA Ops:
  0.0 62.6 %shard_map.55 = bf16[1,2,512,512]{3,2,1,0:T(8,128)(2,1)S(1)} custom-call(bf16[1,2,512,512]{3,2,1,0:T(8,128)(2,1)} %facets.1, s32[4]{0:T(128)} %offsets_in.1, f32[2,32,128]{2,1,0:T(8,128)} %vis.1, f32[32,128]{1,0:T(8,128)} %weights_in.1, s32[32,128]{1,0:T(8,128)} %mask_in.1), custom_call_target="tpu_custom_call" | custom-call | flops 2147483648 | bytes 2097152 | tf_op jit(solution)/shard_map/pallas_call | solution.py:418
  62.6 1.0 %copy.7 = bf16[1,2,512,512]{3,2,1,0:T(8,128)(2,1)} copy(bf16[1,2,512,512]{3,2,1,0:T(8,128)(2,1)S(1)} %shard_map.55) | data formatting | bytes 2097152

commit v5 on v4

--- a/solution.py
+++ b/solution.py
@@ -160,11 +160,6 @@
     send_factor = pltpu.make_async_remote_copy(
         src_ref=factor, dst_ref=factor_here, send_sem=v_send.at[1], recv_sem=v_recv.at[1], device_id=(t, f), device_id_type=MESH)
 
-    @pl.when(apart)
-    def _():
-        send_vis.start()
-        send_factor.start()
-
     @pl.when(jnp.logical_not(apart))
     def _():
         get_vis.start()
@@ -197,8 +192,14 @@
             phase[0, s] = cos_value
             phase[1, s] = sin_value
 
-    for p in range(PASSES):
-        join(p)
+    join(0)
+
+    @pl.when(apart)
+    def _():
+        send_vis.start()
+        send_factor.start()
+
+    join(1)
 
     def psi(r, s):
         j = lax.broadcasted_iota(jnp.int32, (1, half), 1)

time: 64.6 us -> 64.1 us (level)
  no operation moved by 1% of the time
where the time goes in v5:
time: 64.1 us; the launch traced here: 63.1 us
  Pallas kernels  62.1 us (97%)
  local copies, waits for them, and re-layouts  0.97 us (2%)
    pallas_call x1, Pallas kernels, on_device(): pl.pallas_call(functools.partial(kernel, nf, ns), out_shape=jax.ShapeDtyp...  62.1 us

profile of v5, /device:TPU:1, one launch (start us, length us, event | category | flops | bytes accessed | tf_op | source)
XLA Modules:
  0.0 63.1 jit_solution(2452248237653062518)
XLA Ops:
  0.0 62.1 %shard_map.55 = bf16[1,2,512,512]{3,2,1,0:T(8,128)(2,1)S(1)} custom-call(bf16[1,2,512,512]{3,2,1,0:T(8,128)(2,1)} %facets.1, s32[4]{0:T(128)} %offsets_in.1, f32[2,32,128]{2,1,0:T(8,128)} %vis.1, f32[32,128]{1,0:T(8,128)} %weights_in.1, s32[32,128]{1,0:T(8,128)} %mask_in.1), custom_call_target="tpu_custom_call" | custom-call | flops 2147483648 | bytes 2097152 | tf_op jit(solution)/shard_map/pallas_call | solution.py:419
  62.1 1.0 %copy.7 = bf16[1,2,512,512]{3,2,1,0:T(8,128)(2,1)} copy(bf16[1,2,512,512]{3,2,1,0:T(8,128)(2,1)S(1)} %shard_map.55) | data formatting | bytes 2097152

commit v6 on v5

--- a/solution.py
+++ b/solution.py
@@ -146,12 +146,11 @@
                 joined(p, way, u).start()
                 if p + 1 < PASSES:
                     relay(p + 1, way, u).start()
-        if p + 1 < PASSES:
-            for n in range(3):
-                direct(p + 1, n).start()
 
     get_mine.wait()
     start_relays(0)
+    for n in range(3):
+        direct(1, n).start()
     get_weights.wait()
     get_mask.wait()
     factor[...] = weights[...] * mask[...].astype(jnp.float32)

time: 64.1 us -> 64.5 us (level)
  no operation moved by 1% of the time
where the time goes in v6:
time: 64.5 us; the launch traced here: 63.5 us
  Pallas kernels  62.5 us (97%)
  local copies, waits for them, and re-layouts  0.97 us (2%)
    pallas_call x1, Pallas kernels, on_device(): pl.pallas_call(functools.partial(kernel, nf, ns), out_shape=jax.ShapeDtyp...  62.5 us

profile of v6, /device:TPU:1, one launch (start us, length us, event | category | flops | bytes accessed | tf_op | source)
XLA Modules:
  0.0 63.5 jit_solution(17767723685300495440)
XLA Ops:
  0.0 62.5 %shard_map.55 = bf16[1,2,512,512]{3,2,1,0:T(8,128)(2,1)S(1)} custom-call(bf16[1,2,512,512]{3,2,1,0:T(8,128)(2,1)} %facets.1, s32[4]{0:T(128)} %offsets_in.1, f32[2,32,128]{2,1,0:T(8,128)} %vis.1, f32[32,128]{1,0:T(8,128)} %weights_in.1, s32[32,128]{1,0:T(8,128)} %mask_in.1), custom_call_target="tpu_custom_call" | custom-call | flops 2147483648 | bytes 2097152 | tf_op jit(solution)/shard_map/pallas_call | solution.py:418
  62.6 1.0 %copy.7 = bf16[1,2,512,512]{3,2,1,0:T(8,128)(2,1)} copy(bf16[1,2,512,512]{3,2,1,0:T(8,128)(2,1)S(1)} %shard_map.55) | data formatting | bytes 2097152
